TPU v7x, 128 devices: a whole 4x4x4 slice. The times are simulated.
128 devices in a mesh: rows: 32 (over x, y, core), rep: 4 (over z).
Axes of the slice: x: 4, y: 4, z: 4, core: 2. Of those that a mesh axis runs over, the one named last changes fastest.
Arguments:
- vectors: bfloat16 [65536, 1024], P(('rows', 'rep')), may hold values from -96 to 96
- list_ids: int32 [65536], P(('rows', 'rep')), may hold values from 0 to 262143, as said below
- centroids: bfloat16 [262144, 1024], P(('rows', 'rep')), may hold values from -16 to 16
- list_place: int32 [262144], replicated, may hold values from 0 to 262143, as said below
- codes_first: int32 [65536, 128], P(('rows', 'rep')), may hold values from 0 to 255
- codes_second: int32 [65536, 128], P(('rows', 'rep')), may hold values from 0 to 255
Outputs:
- codebook_first: float32 [256, 1024], P(None, 'rows')
- codebook_second: float32 [256, 1024], P(None, 'rows')
Inputs may be any that keep to these rules, and one draw needn't show every extreme that they name: list_place is a permutation of the table rows. Among the rows of one device, at most 8 have list_place[list_ids] inside one device's block of 2048 table rows, and exactly 8 for some blocks of every device.
All inputs are finite; a program needn't handle non-finite values.
Results may differ from a plain program's by a relative error of at most 0.0003.
Values may be sent and summed in bfloat16 or wider, within the bound.
A program may use at most 64 MiB of HBM per device.

v0:
```python
import math
import jax
import jax.numpy as jnp
from jax import lax
from jax.sharding import PartitionSpec as P

SUB = 8
K = 256


def code_sums(residual, code_pair):
    total_rows = residual.shape[0]
    subspaces = code_pair[0].shape[1]
    block_rows = math.gcd(total_rows, 32768 // subspaces)
    turn_count = total_rows // block_rows
    shaped = residual.reshape(turn_count, block_rows, subspaces, SUB)
    codewords = jnp.arange(K, dtype=jnp.int32)
    zeros_sums = jnp.zeros((subspaces, K, SUB), jnp.float32)
    zeros_counts = jnp.zeros((subspaces, K), jnp.float32)

    def add_block(running, block_index):
        row_block = lax.dynamic_index_in_dim(shaped, block_index, 0, keepdims=False)
        updated = []
        for code_all, state in zip(code_pair, running):
            code_block = lax.dynamic_slice_in_dim(code_all, block_index * block_rows, block_rows, 0)
            one_hot = (code_block[:, :, None] == codewords).astype(row_block.dtype)
            block_sums = jnp.einsum(
                "rsk,rsc->skc",
                one_hot,
                row_block,
                preferred_element_type=jnp.float32,
                precision=lax.Precision.HIGHEST,
            )
            block_counts = jnp.sum(one_hot, axis=0, dtype=jnp.float32)
            updated.append((state[0] + block_sums, state[1] + block_counts))
        return (tuple(updated), None)

    start_state = ((zeros_sums, zeros_counts), (zeros_sums, zeros_counts))
    final_state, unused = lax.scan(add_block, start_state, jnp.arange(turn_count, dtype=jnp.int32))
    laid_out = []
    for sums_part, counts_part in final_state:
        laid_out.append(jnp.transpose(sums_part, (1, 0, 2)).reshape(K, subspaces * SUB))
        laid_out.append(counts_part.T)
    return tuple(laid_out)


def finish(first_sums, first_counts, second_sums, second_counts):
    totals = lax.psum((first_sums, first_counts, second_sums, second_counts), "rep")
    codebooks = []
    for sums_part, counts_part in ((totals[0], totals[1]), (totals[2], totals[3])):
        spread = jnp.repeat(jnp.maximum(counts_part, 1.0), SUB, axis=1)
        codebooks.append(sums_part / spread)
    return (codebooks[0], codebooks[1])


def plan_slots(list_ids, list_place, shard_rows, devices, capacity):
    local_rows = list_ids.shape[0]
    places = jnp.take(list_place, list_ids, axis=0)
    owner_ids = places // shard_rows
    slot_in = places - owner_ids * shard_rows
    by_owner = jnp.argsort(owner_ids, stable=True)
    sorted_owner = owner_ids[by_owner]
    per_owner = jnp.sum(
        (owner_ids[:, None] == jnp.arange(devices, dtype=jnp.int32)[None, :]).astype(jnp.int32),
        axis=0,
    )
    first_row = jnp.cumsum(per_owner) - per_owner
    rank_sorted = jnp.arange(local_rows, dtype=jnp.int32) - first_row[sorted_owner]
    position = (
        jnp.zeros((local_rows,), jnp.int32).at[by_owner].set(sorted_owner * capacity + rank_sorted)
    )
    request = (
        jnp.zeros((devices * capacity,), jnp.int32)
        .at[position]
        .set(slot_in)
        .reshape(devices, capacity)
    )
    return (position, request)


def fetch_residual(vectors, centroids, position, request, devices, capacity):
    wanted_ids = lax.all_to_all(request, ("rows", "rep"), split_axis=0, concat_axis=0, tiled=True)
    answer = jnp.take(centroids, wanted_ids.reshape(-1), axis=0)
    answer = answer.reshape(wanted_ids.shape[0], wanted_ids.shape[1], centroids.shape[1])
    fetched = lax.all_to_all(answer, ("rows", "rep"), split_axis=0, concat_axis=0, tiled=True)
    fetched_rows = jnp.take(
        fetched.reshape(devices * capacity, centroids.shape[1]), position, axis=0
    )
    return vectors.astype(jnp.float32) - fetched_rows.astype(jnp.float32)


def on_device(vectors, list_ids, centroids, list_place, codes_first, codes_second):
    devices = lax.axis_size(("rows", "rep"))
    local_rows = vectors.shape[0]
    shard_rows = centroids.shape[0]
    capacity = 2 * local_rows // devices
    position, request = plan_slots(list_ids, list_place, shard_rows, devices, capacity)
    residual = fetch_residual(vectors, centroids, position, request, devices, capacity)
    transposed = (
        lax.all_to_all(residual, "rows", split_axis=1, concat_axis=0, tiled=True),
        lax.all_to_all(codes_first, "rows", split_axis=1, concat_axis=0, tiled=True),
        lax.all_to_all(codes_second, "rows", split_axis=1, concat_axis=0, tiled=True),
    )
    local_parts = code_sums(transposed[0], (transposed[1], transposed[2]))
    return finish(local_parts[0], local_parts[1], local_parts[2], local_parts[3])


def solution(mesh):
    return jax.shard_map(
        on_device,
        mesh=mesh,
        in_specs=(
            P(("rows", "rep"), None),
            P(("rows", "rep")),
            P(("rows", "rep"), None),
            P(),
            P(("rows", "rep"), None),
            P(("rows", "rep"), None),
        ),
        out_specs=(P(None, "rows"), P(None, "rows")),
        check_vma=False,
    )
```

profile of v0, /device:TPU:0, one launch (start us, length us, event | category | flops | bytes accessed | tf_op | source)
XLA Modules:
  0.0 313.5 jit_solution(9564695646376202633)
XLA Ops:
  7.2 0.0 copy-start
  7.2 0.8 compare_select_fusion.5
  8.0 0.4 copy-done
  8.4 3.1 gather_fusion
  11.6 0.1 convert_reduce_fusion
  11.7 0.1 copy.25
  11.8 0.2 reduce-window.9
  12.0 0.1 reduce
  12.2 3.8 %sort.17 = (s32[512]{0:T(512)}, s32[512]{0:T(512)S(1)}) sort(s32[512]{0:T(512)S(1)} %get-tuple-element.172, s32[512]{0:T(512)S(1)} %iota.21), dimensions={0}, to_apply=%region_0.1 | sort | flops 4608 | bytes 8192 | tf_op jit(solution)/shard_map/jit(argsort)/sort | solution.py:61
  15.9 3.5 %gather_fusion.1 = s32[512]{0:T(512)S(1)} fusion(s32[512]{0:T(512)S(1)} %get-tuple-element.172, s32[1024]{0:T(1024)S(1)} %pad_clamp_fusion.2), kind=kCustom, calls=%fused_computation.1 | custom fusion | bytes 6144 | tf_op jit(solution)/shard_map/gather | solution.py:62
  19.5 3.3 %gather_fusion.2 = s32[512]{0:T(512)S(1)} fusion(s32[128]{0:T(128)S(1)} %sub.19, s32[1024]{0:T(1024)S(1)} %pad_clamp_fusion.1), kind=kCustom, calls=%fused_computation.2 | custom fusion | bytes 6144 | tf_op jit(solution)/shard_map/gather | solution.py:68
  22.8 2.4 scatter_custom_fusion
  25.3 2.4 scatter_custom_fusion.1
  27.7 0.1 all_to_all.53
  27.8 20.0 %all_to_all.68 = s32[128,1,8]{2,1,0:T(1,128)S(1)} all-to-all(s32[128,1,8]{2,1,0:T(1,128)S(1)} %bitcast.51), channel_id=1, replica_groups=mesh['rows'=32,'rep'=4] {'rows','rep'}, dimensions={0} | all-to-all | bytes 8192 | tf_op jit(solution)/shard_map/all_to_all | solution.py:82
  47.8 0.5 broadcast.159
  48.3 0.8 reduce.4
  49.2 0.1 reshape.157
  49.3 7.7 %gather_fusion.3 = bf16[1024,1024]{1,0:T(8,128)(2,1)S(1)} fusion(bf16[2048,1024]{1,0:T(8,128)(2,1)} %param.10, s32[1024]{0:T(1024)S(1)} %broadcast_clamp_fusion), kind=kCustom, calls=%fused_computation.3 | custom fusion | bytes 4198400 | tf_op jit(solution)/shard_map/jit(_take)/gather | solution.py:83
  57.0 1.6 bitcast_select_fusion
  58.7 4.9 %all-to-all-start.2 = ((bf16[128,8,1024]{2,1,0:T(8,128)(2,1)}), bf16[128,8,1024]{2,1,0:T(8,128)(2,1)S(1)}, u32[]{:S(2)}, u32[]{:S(2)}) async-start(bf16[128,8,1024]{2,1,0:T(8,128)(2,1)} %bitcast_select_fusion), calls=%async_computation.2 | async-start | bytes 4194304 | tf_op jit(solution)/shard_map/all_to_all | solution.py:85
  63.6 1.1 copy.24
  64.6 0.8 all_to_all.49
  65.5 28.3 %all-to-all-done.2 = bf16[128,8,1024]{2,1,0:T(8,128)(2,1)S(1)} async-done(((bf16[128,8,1024]{2,1,0:T(8,128)(2,1)}), bf16[128,8,1024]{2,1,0:T(8,128)(2,1)S(1)}, u32[]{:S(2)}, u32[]{:S(2)}) %all-to-all-start.2) | async-done | bytes 2097184 | tf_op jit(solution)/shard_map/all_to_all | solution.py:85
  93.7 3.9 %all-to-all-start = ((s32[512,32,4]{0,2,1:T(4,128)}), s32[512,32,4]{0,2,1:T(4,128)S(1)}, u32[]{:S(2)}, u32[]{:S(2)}) async-start(s32[512,32,4]{0,2,1:T(4,128)} %all_to_all.49), calls=%async_computation | async-start | bytes 524288 | tf_op jit(solution)/shard_map/all_to_all | solution.py:101
  97.6 2.8 gather_fusion.4
  100.4 1.9 convert_subtract_fusion
  102.3 1.9 copy.27
  104.2 2.4 all-to-all-done
  106.5 5.0 %all-to-all-start.3 = ((f32[512,32,32]{0,2,1:T(8,128)}), f32[512,32,32]{0,2,1:T(8,128)S(1)}, u32[]{:S(2)}, u32[]{:S(2)}) async-start(f32[512,32,32]{0,2,1:T(8,128)} %bitcast.48), calls=%async_computation.3 | async-start | bytes 4194304 | tf_op jit(solution)/shard_map/all_to_all | solution.py:100
  111.5 1.8 copy.29
  113.4 1.7 all_to_all.59
  115.1 25.4 %all-to-all-done.3 = f32[512,32,32]{0,2,1:T(8,128)S(1)} async-done(((f32[512,32,32]{0,2,1:T(8,128)}), f32[512,32,32]{0,2,1:T(8,128)S(1)}, u32[]{:S(2)}, u32[]{:S(2)}) %all-to-all-start.3) | async-done | bytes 2097184 | tf_op jit(solution)/shard_map/all_to_all | solution.py:100
  140.5 4.6 %all-to-all-start.4 = ((s32[512,32,4]{0,2,1:T(4,128)}), s32[512,32,4]{0,2,1:T(4,128)}, u32[]{:S(2)}, u32[]{:S(2)}) async-start(s32[512,32,4]{0,2,1:T(4,128)} %all_to_all.59), calls=%async_computation.4 | async-start | bytes 524288 | tf_op jit(solution)/shard_map/all_to_all | solution.py:102
  145.1 0.2 all-reduce.3.cloned.1.call-start
  145.3 2.5 copy.28
  147.8 4.0 %reshape.159 = f32[2,8192,4,8]{1,0,3,2:T(2,128)} reshape(f32[32,512,32]{1,0,2:T(8,128)} %copy.28) | data formatting | bytes 4194304 | tf_op jit(solution)/shard_map/reshape | solution.py:16
  151.9 2.1 all-to-all-done.4
  154.0 111.4 %while.18 = (s32[]{:T(128)}, f32[4,256,8]{1,2,0:T(8,128)S(1)}, f32[4,256]{1,0:T(4,128)S(1)}, f32[4,256,8]{1,2,0:T(8,128)S(1)}, f32[4,256]{1,0:T(4,128)S(1)}, /*i...) while((s32[]{:T(128)}, f32[4,256,8]{1,2,0:T(8,128)S(1)}, ...), condition=%wide.region_8.9_spmd.clone.clone, body=%wide.region_5.8_spmd.clone.clone.sunk | while | flops 1677756416 | bytes 5406969 | solution.py:39
  154.0 0.6 dynamic_slice.32
  155.2 0.9 constant_dynamic-slice_fusion.8
  158.1 2.7 constant_dynamic-slice_fusion.7
  160.8 10.9 %fusion.25 = f32[4,256,8]{1,2,0:T(8,128)S(1)} fusion(s32[8192,4]{0,1:T(4,128)S(1)} %constant_dynamic-slice_fusion.8, f32[1,8192,4,8]{1,0,3,2:T(1,128)S(1)} %constant_dynamic-slice_fusion.7, f32[4,256,8]{1,2,0:T(8,128)S(1)} %get-tuple-element.253, pred[]{:T(512)S(6)} %compare.12), kind=kOutput, calls=%fused_computation.18.clone.1 | convolution fusion | flops 813711360 | bytes 1245185 | tf_op jit(solution)/shard_map/while/body/eval_jaxpr/rsk,rsc->skc/dot_general | solution.py:27
  171.7 10.9 %fusion.22 = f32[4,256,8]{1,2,0:T(8,128)S(1)} fusion(s32[8192,4]{0,1:T(4,128)S(1)} %constant_dynamic-slice_fusion.6, f32[1,8192,4,8]{1,0,3,2:T(1,128)S(1)} %constant_dynamic-slice_fusion.7, f32[4,256,8]{1,2,0:T(8,128)S(1)} %get-tuple-element.251, pred[]{:T(512)S(6)} %compare.12), kind=kOutput, calls=%fused_computation.19.clone.1 | convolution fusion | flops 813711360 | bytes 1245185 | tf_op jit(solution)/shard_map/while/body/eval_jaxpr/rsk,rsc->skc/dot_general | solution.py:27
  182.5 13.5 %fusion.23 = f32[4,256]{1,0:T(4,128)S(1)} fusion(s32[8192,4]{0,1:T(4,128)S(1)} %constant_dynamic-slice_fusion.8), kind=kLoop, calls=%fused_computation.14.clone.1 | loop fusion | flops 25164800 | bytes 135168 | tf_op jit(solution)/shard_map/while/body/eval_jaxpr/reduce_sum | solution.py:34
  196.1 13.6 %fusion.24 = f32[4,256]{1,0:T(4,128)S(1)} fusion(s32[8192,4]{0,1:T(4,128)S(1)} %constant_dynamic-slice_fusion.6), kind=kLoop, calls=%fused_computation.15.clone.1 | loop fusion | flops 25164800 | bytes 135168 | tf_op jit(solution)/shard_map/while/body/eval_jaxpr/reduce_sum | solution.py:34
  209.7 0.6 dynamic_slice.32
  211.0 0.9 constant_dynamic-slice_fusion.8
  213.8 2.7 constant_dynamic-slice_fusion.7
  216.5 10.9 %fusion.25 = f32[4,256,8]{1,2,0:T(8,128)S(1)} fusion(s32[8192,4]{0,1:T(4,128)S(1)} %constant_dynamic-slice_fusion.8, f32[1,8192,4,8]{1,0,3,2:T(1,128)S(1)} %constant_dynamic-slice_fusion.7, f32[4,256,8]{1,2,0:T(8,128)S(1)} %get-tuple-element.253, pred[]{:T(512)S(6)} %compare.12), kind=kOutput, calls=%fused_computation.18.clone.1 | convolution fusion | flops 813711360 | bytes 1245185 | tf_op jit(solution)/shard_map/while/body/eval_jaxpr/rsk,rsc->skc/dot_general | solution.py:27
  227.4 10.9 %fusion.22 = f32[4,256,8]{1,2,0:T(8,128)S(1)} fusion(s32[8192,4]{0,1:T(4,128)S(1)} %constant_dynamic-slice_fusion.6, f32[1,8192,4,8]{1,0,3,2:T(1,128)S(1)} %constant_dynamic-slice_fusion.7, f32[4,256,8]{1,2,0:T(8,128)S(1)} %get-tuple-element.251, pred[]{:T(512)S(6)} %compare.12), kind=kOutput, calls=%fused_computation.19.clone.1 | convolution fusion | flops 813711360 | bytes 1245185 | tf_op jit(solution)/shard_map/while/body/eval_jaxpr/rsk,rsc->skc/dot_general | solution.py:27
  238.3 13.5 %fusion.23 = f32[4,256]{1,0:T(4,128)S(1)} fusion(s32[8192,4]{0,1:T(4,128)S(1)} %constant_dynamic-slice_fusion.8), kind=kLoop, calls=%fused_computation.14.clone.1 | loop fusion | flops 25164800 | bytes 135168 | tf_op jit(solution)/shard_map/while/body/eval_jaxpr/reduce_sum | solution.py:34
  251.8 13.6 %fusion.24 = f32[4,256]{1,0:T(4,128)S(1)} fusion(s32[8192,4]{0,1:T(4,128)S(1)} %constant_dynamic-slice_fusion.6), kind=kLoop, calls=%fused_computation.15.clone.1 | loop fusion | flops 25164800 | bytes 135168 | tf_op jit(solution)/shard_map/while/body/eval_jaxpr/reduce_sum | solution.py:34
  265.4 0.0 copy-start.3
  265.5 0.0 copy-start.4
  265.5 0.6 copy-done.1
  266.0 0.0 copy-done.2
  266.0 0.0 copy-done.3
  266.1 0.0 copy-done.4
  266.1 0.0 all-reduce.3.cloned.1.call-update
  266.1 37.8 %all-reduce.3.cloned.1.call-done = (f32[256,32]{0,1:T(8,128)}, f32[256,4]{0,1:T(4,128)}, f32[256,32]{0,1:T(8,128)}, f32[256,4]{0,1:T(4,128)}) async-done(((f32[256,32]{0,1:T(8,128)}, f32[256,4]{0,1:T(4,128)}, f32[256,32]{0,1:T(8,128)}, f32[256,4]{0,1:T(4,128)}), (f32[256,32]{0,1:T(8,128)}, f32[256,4]{0,1:T(4,128)}, f32[256,32]{0,1:T(8,128)}, f32[256,4]{0,1:T(4,128)})) %all-reduce.3.cloned.1.call-update) | async-done | bytes 73744 | tf_op jit(solution)/shard_map/psum | solution.py:48
  303.9 0.7 broadcast_maximum_fusion
  304.6 0.7 broadcast_maximum_fusion.1
  305.2 1.4 bitcast_divide_fusion
  (28 shorter events, 0.2 us)
Async XLA Ops:
  7.2 1.2 copy-start
  7.2 4.4 %copy-start.5 = (s32[512]{0:T(512)S(1)}, s32[512]{0:T(512)}, u32[]{:S(2)}) copy-start(s32[512]{0:T(512)} %param.9) | copy-start | bytes 6148
  58.7 35.1 %all-to-all-start.2 = ((bf16[128,8,1024]{2,1,0:T(8,128)(2,1)}), bf16[128,8,1024]{2,1,0:T(8,128)(2,1)S(1)}, u32[]{:S(2)}, u32[]{:S(2)}) async-start(bf16[128,8,1024]{2,1,0:T(8,128)(2,1)} %bitcast_select_fusion), calls=%async_computation.2 | async-start | bytes 4194304 | tf_op jit(solution)/shard_map/all_to_all | solution.py:85
  93.7 12.8 %all-to-all-start = ((s32[512,32,4]{0,2,1:T(4,128)}), s32[512,32,4]{0,2,1:T(4,128)S(1)}, u32[]{:S(2)}, u32[]{:S(2)}) async-start(s32[512,32,4]{0,2,1:T(4,128)} %all_to_all.49), calls=%async_computation | async-start | bytes 524288 | tf_op jit(solution)/shard_map/all_to_all | solution.py:101
  106.5 33.9 %all-to-all-start.3 = ((f32[512,32,32]{0,2,1:T(8,128)}), f32[512,32,32]{0,2,1:T(8,128)S(1)}, u32[]{:S(2)}, u32[]{:S(2)}) async-start(f32[512,32,32]{0,2,1:T(8,128)} %bitcast.48), calls=%async_computation.3 | async-start | bytes 4194304 | tf_op jit(solution)/shard_map/all_to_all | solution.py:100
  140.5 13.5 %all-to-all-start.4 = ((s32[512,32,4]{0,2,1:T(4,128)}), s32[512,32,4]{0,2,1:T(4,128)}, u32[]{:S(2)}, u32[]{:S(2)}) async-start(s32[512,32,4]{0,2,1:T(4,128)} %all_to_all.59), calls=%async_computation.4 | async-start | bytes 524288 | tf_op jit(solution)/shard_map/all_to_all | solution.py:102
  145.1 158.8 %all-reduce.3.cloned.1.call-start = ((), (), s32[]{:S(2)}) async-start(), calls=%async_computation.5 | async-start | bytes 147456 | tf_op jit(solution)/shard_map/psum | solution.py:48
  265.4 0.6 copy-start.1
  265.4 0.6 copy-start.2
  265.4 0.6 copy-start.3
  265.5 0.6 copy-start.4
Sparse Core Ops, SparseCore 0:
  266.2 37.6 all-reduce.2
where the time goes:
time: 314 us
  waiting for transfers between devices  95.9 us (31%)
  other arithmetic  66.5 us (21%)
  local copies, waits for them, and re-layouts  49.5 us (16%)
  matrix products  43.4 us (14%)
  blocking collectives  20 us (6%)
  starting transfers between devices  18.6 us (6%)
  between operations  14.3 us (5%)
  loops' own time  5.27 us (2%)
    reduce_sum x4, other arithmetic, add_block(): block_counts = jnp.sum(one_hot, axis=0, dtype=jnp.float32)  54.3 us
    dot_general x4, matrix products, add_block(): jnp.einsum('rsk,rsc->skc', one_hot, row_block, preferred_element_type=jnp...  43.4 us
    psum x1, waiting for transfers between devices, finish(): lax.psum((first_sums, first_counts, second_sums, second_counts), 'rep')  37.8 us
    all_to_all x1, waiting for transfers between devices, fetch_residual(): lax.all_to_all(answer, ('rows', 'rep'), split_axis=0, concat_axis=0, tile...  28.3 us
    all_to_all x1, waiting for transfers between devices, on_device(): lax.all_to_all(residual, 'rows', split_axis=1, concat_axis=0, tiled=True)  25.4 us
    all_to_all x1, blocking collectives, fetch_residual(): lax.all_to_all(request, ('rows', 'rep'), split_axis=0, concat_axis=0, til...  20 us
    gather x1, local copies, waits for them, and re-layouts, fetch_residual(): answer = jnp.take(centroids, wanted_ids.reshape(-1), axis=0)  7.71 us
  transfers between devices with their start and end apart: 5, of which 5 were waited for; matrix products, arithmetic and copies ran while one was open for 5% of the time, Pallas kernels for 0%

commit v1 on v0

--- a/solution.py
+++ b/solution.py
@@ -1,3 +1,4 @@
+import functools
 import math
 import jax
 import jax.numpy as jnp
@@ -6,6 +7,17 @@
 
 SUB = 8
 K = 256
+
+
+def see_cycles(raw, array_dim, dim_k):
+    work_now = jnp.concatenate(
+        lax.all_to_all(jnp.stack(jnp.split(raw, lax.axis_size("rows"), array_dim)), "rows", 0, 0),
+        dim_k,
+    )
+    return work_now
+
+
+build_the_zone = functools.partial(see_cycles, array_dim=1, dim_k=0)
 
 
 def code_sums(residual, code_pair):
@@ -98,7 +110,7 @@
     residual = fetch_residual(vectors, centroids, position, request, devices, capacity)
     transposed = (
         lax.all_to_all(residual, "rows", split_axis=1, concat_axis=0, tiled=True),
-        lax.all_to_all(codes_first, "rows", split_axis=1, concat_axis=0, tiled=True),
+        build_the_zone(codes_first),
         lax.all_to_all(codes_second, "rows", split_axis=1, concat_axis=0, tiled=True),
     )
     local_parts = code_sums(transposed[0], (transposed[1], transposed[2]))

time: 314 us -> 343 us (1.092)
  local copies, waits for them, and re-layouts: 49.5 us -> 99 us
  waiting for transfers between devices: 95.9 us -> 69.9 us
    another operation x1 -> x37, local copies, waits for them, and re-layouts: 0.12 us -> 51.5 us  [the longest x36 51.3 us: see_cycles(): jnp.stack(jnp.split(raw, lax.axis_size('rows'), array_dim))]
    all_to_all x1, waiting for transfers between devices: 28.3 us -> 0.01 us  [fetch_residual(): lax.all_to_all(answer, ('rows', 'rep'), split_axis=0, concat_axis=0, tile...]
  transfers between devices with their start and end apart: 5 -> 5, of which waited for: 5 -> 4; matrix products, arithmetic and copies ran while one was open for 5% -> 20% of each run, Pallas kernels for 0% -> 0%
where the time goes in v1:
time: 343 us; the launch traced here: 341 us
  local copies, waits for them, and re-layouts  99 us (29%)
  waiting for transfers between devices  69.9 us (20%)
  other arithmetic  67.8 us (20%)
  matrix products  43.4 us (13%)
  starting transfers between devices  21.3 us (6%)
  blocking collectives  20 us (6%)
  between operations  14.4 us (4%)
  loops' own time  5.27 us (2%)
    reduce_sum x4, other arithmetic, add_block(): block_counts = jnp.sum(one_hot, axis=0, dtype=jnp.float32)  54.3 us
    another operation x36, local copies, waits for them, and re-layouts, see_cycles(): jnp.stack(jnp.split(raw, lax.axis_size('rows'), array_dim))  51.3 us
    dot_general x4, matrix products, add_block(): jnp.einsum('rsk,rsc->skc', one_hot, row_block, preferred_element_type=jnp...  43.4 us
    psum x1, waiting for transfers between devices, finish(): lax.psum((first_sums, first_counts, second_sums, second_counts), 'rep')  40 us
    all_to_all x1, waiting for transfers between devices, on_device(): lax.all_to_all(residual, 'rows', split_axis=1, concat_axis=0, tiled=True)  25.4 us
    all_to_all x1, blocking collectives, fetch_residual(): lax.all_to_all(request, ('rows', 'rep'), split_axis=0, concat_axis=0, til...  20 us
    gather x1, local copies, waits for them, and re-layouts, fetch_residual(): answer = jnp.take(centroids, wanted_ids.reshape(-1), axis=0)  7.71 us
  transfers between devices with their start and end apart: 5, of which 4 were waited for; matrix products, arithmetic and copies ran while one was open for 20% of the time, Pallas kernels for 0%

profile of v1, /device:TPU:0, one launch (start us, length us, event | category | flops | bytes accessed | tf_op | source)
XLA Modules:
  0.0 341.0 jit_solution(1596736396713728341)
XLA Ops:
  8.4 3.1 gather_fusion
  12.2 3.8 %sort.17 = (s32[512]{0:T(512)}, s32[512]{0:T(512)S(1)}) sort(s32[512]{0:T(512)S(1)} %get-tuple-element.172, s32[512]{0:T(512)S(1)} %iota.21), dimensions={0}, to_apply=%region_0.1 | sort | flops 4608 | bytes 8192 | tf_op jit(solution)/shard_map/jit(argsort)/sort | solution.py:73
  15.9 3.5 %gather_fusion.1 = s32[512]{0:T(512)S(1)} fusion(s32[512]{0:T(512)S(1)} %get-tuple-element.172, s32[1024]{0:T(1024)S(1)} %pad_clamp_fusion.2), kind=kCustom, calls=%fused_computation.1 | custom fusion | bytes 6144 | tf_op jit(solution)/shard_map/gather | solution.py:74
  19.5 3.3 gather_fusion.2
  22.8 2.4 scatter_custom_fusion
  25.3 2.4 scatter_custom_fusion.1
  27.9 20.0 %all_to_all.54 = s32[128,1,8]{2,1,0:T(1,128)S(1)} all-to-all(s32[128,1,8]{2,1,0:T(1,128)S(1)} %bitcast.111), channel_id=1, replica_groups=mesh['rows'=32,'rep'=4] {'rows','rep'}, dimensions={0} | all-to-all | bytes 8192 | tf_op jit(solution)/shard_map/all_to_all | solution.py:94
  49.4 7.7 %gather_fusion.3 = bf16[1024,1024]{1,0:T(8,128)(2,1)S(1)} fusion(bf16[2048,1024]{1,0:T(8,128)(2,1)} %param.10, s32[1024]{0:T(1024)S(1)} %broadcast_clamp_fusion), kind=kCustom, calls=%fused_computation.3 | custom fusion | bytes 4198400 | tf_op jit(solution)/shard_map/jit(_take)/gather | solution.py:95
  57.1 1.6 bitcast_select_fusion
  58.7 4.9 %all-to-all-start.2 = ((bf16[128,8,1024]{2,1,0:T(8,128)(2,1)}), bf16[128,8,1024]{2,1,0:T(8,128)(2,1)S(1)}, u32[]{:S(2)}, u32[]{:S(2)}) async-start(bf16[128,8,1024]{2,1,0:T(8,128)(2,1)} %bitcast_select_fusion), calls=%async_computation.2 | async-start | bytes 4194304 | tf_op jit(solution)/shard_map/all_to_all | solution.py:97
  63.6 3.6 %slice_bitcast_fusion = (s32[1,512,4]{2,1,0:T(8,128)}, s32[1,512,4]{2,1,0:T(8,128)}, s32[1,512,4]{2,1,0:T(8,128)}, s32[1,512,4]{2,1,0:T(8,128)}, s32[1,512,4]{2,...) fusion(s32[512,128]{1,0:T(8,128)S(1)} %copy-done.1), kind=kLoop, calls=%fused_computation.30 | loop fusion | bytes 311296 | tf_op jit(solution)/shard_map/stack | solution.py:14
  68.3 1.1 copy.142
  69.3 1.1 copy.143
  70.4 1.1 copy.144
  71.5 1.1 copy.145
  72.5 1.1 copy.146
  73.6 1.1 copy.147
  74.7 1.1 copy.148
  75.7 1.1 copy.149
  76.8 1.1 copy.150
  77.9 1.1 copy.151
  81.1 1.1 copy.154
  84.3 1.1 copy.157
  86.4 1.7 copy.159
  88.1 2.6 slice_bitcast_fusion.19
  90.7 1.7 copy.128
  92.4 1.7 copy.129
  94.1 1.7 copy.130
  95.8 1.7 copy.131
  97.4 1.7 copy.132
  99.1 1.7 copy.133
  100.7 1.7 copy.134
  102.4 1.7 copy.135
  104.0 1.7 copy.136
  105.7 1.6 copy.137
  107.3 1.7 copy.138
  109.0 1.7 copy.139
  111.4 2.7 stack.131
  116.3 6.7 %all-to-all-start = ((s32[32,512,4]{1,2,0:T(4,128)}), s32[32,512,4]{1,2,0:T(4,128)S(1)}, u32[]{:S(2)}, u32[]{:S(2)}) async-start(s32[32,512,4]{1,2,0:T(4,128)} %copy.88), calls=%async_computation | async-start | bytes 524288 | tf_op jit(solution)/shard_map/all_to_all | solution.py:14
  123.1 2.8 gather_fusion.4
  125.9 1.9 convert_subtract_fusion
  127.8 1.9 copy.91
  129.7 2.2 all-to-all-done
  131.8 5.0 %all-to-all-start.3 = ((f32[512,32,32]{0,2,1:T(8,128)}), f32[512,32,32]{0,2,1:T(8,128)S(1)}, u32[]{:S(2)}, u32[]{:S(2)}) async-start(f32[512,32,32]{0,2,1:T(8,128)} %bitcast.108), calls=%async_computation.3 | async-start | bytes 4194304 | tf_op jit(solution)/shard_map/all_to_all | solution.py:112
  136.9 1.8 copy.93
  138.7 1.7 all_to_all.45
  140.4 25.4 %all-to-all-done.3 = f32[512,32,32]{0,2,1:T(8,128)S(1)} async-done(((f32[512,32,32]{0,2,1:T(8,128)}), f32[512,32,32]{0,2,1:T(8,128)S(1)}, u32[]{:S(2)}, u32[]{:S(2)}) %all-to-all-start.3) | async-done | bytes 2097184 | tf_op jit(solution)/shard_map/all_to_all | solution.py:112
  165.8 4.6 %all-to-all-start.4 = ((s32[512,32,4]{0,2,1:T(4,128)}), s32[512,32,4]{0,2,1:T(4,128)}, u32[]{:S(2)}, u32[]{:S(2)}) async-start(s32[512,32,4]{0,2,1:T(4,128)} %all_to_all.45), calls=%async_computation.4 | async-start | bytes 524288 | tf_op jit(solution)/shard_map/all_to_all | solution.py:114
  170.5 2.5 copy.92
  173.0 4.0 %reshape.160 = f32[2,8192,4,8]{1,0,3,2:T(2,128)} reshape(f32[32,512,32]{1,0,2:T(8,128)} %copy.92) | data formatting | bytes 4194304 | tf_op jit(solution)/shard_map/reshape | solution.py:28
  177.0 2.3 all-to-all-done.4
  179.3 111.4 %while.18 = (s32[]{:T(128)}, f32[4,256,8]{1,2,0:T(8,128)S(1)}, f32[4,256]{1,0:T(4,128)S(1)}, f32[4,256,8]{1,2,0:T(8,128)S(1)}, f32[4,256]{1,0:T(4,128)S(1)}, /*i...) while((s32[]{:T(128)}, f32[4,256,8]{1,2,0:T(8,128)S(1)}, ...), condition=%wide.region_8.9_spmd.clone.clone, body=%wide.region_5.8_spmd.clone.clone.sunk | while | flops 1677756416 | bytes 5406969 | solution.py:51
  183.4 2.7 constant_dynamic-slice_fusion.7
  186.1 10.9 %fusion.25 = f32[4,256,8]{1,2,0:T(8,128)S(1)} fusion(s32[8192,4]{0,1:T(4,128)S(1)} %constant_dynamic-slice_fusion.8, f32[1,8192,4,8]{1,0,3,2:T(1,128)S(1)} %constant_dynamic-slice_fusion.7, f32[4,256,8]{1,2,0:T(8,128)S(1)} %get-tuple-element.285, pred[]{:T(512)S(6)} %compare.12), kind=kOutput, calls=%fused_computation.18.clone.1 | convolution fusion | flops 813711360 | bytes 1245185 | tf_op jit(solution)/shard_map/while/body/eval_jaxpr/rsk,rsc->skc/dot_general | solution.py:39
  197.0 10.9 %fusion.22 = f32[4,256,8]{1,2,0:T(8,128)S(1)} fusion(s32[8192,4]{0,1:T(4,128)S(1)} %constant_dynamic-slice_fusion.6, f32[1,8192,4,8]{1,0,3,2:T(1,128)S(1)} %constant_dynamic-slice_fusion.7, f32[4,256,8]{1,2,0:T(8,128)S(1)} %get-tuple-element.283, pred[]{:T(512)S(6)} %compare.12), kind=kOutput, calls=%fused_computation.19.clone.1 | convolution fusion | flops 813711360 | bytes 1245185 | tf_op jit(solution)/shard_map/while/body/eval_jaxpr/rsk,rsc->skc/dot_general | solution.py:39
  207.9 13.5 %fusion.23 = f32[4,256]{1,0:T(4,128)S(1)} fusion(s32[8192,4]{0,1:T(4,128)S(1)} %constant_dynamic-slice_fusion.8), kind=kLoop, calls=%fused_computation.14.clone.1 | loop fusion | flops 25164800 | bytes 135168 | tf_op jit(solution)/shard_map/while/body/eval_jaxpr/reduce_sum | solution.py:46
  221.4 13.6 %fusion.24 = f32[4,256]{1,0:T(4,128)S(1)} fusion(s32[8192,4]{0,1:T(4,128)S(1)} %constant_dynamic-slice_fusion.6), kind=kLoop, calls=%fused_computation.15.clone.1 | loop fusion | flops 25164800 | bytes 135168 | tf_op jit(solution)/shard_map/while/body/eval_jaxpr/reduce_sum | solution.py:46
  239.1 2.7 constant_dynamic-slice_fusion.7
  241.8 10.9 %fusion.25 = f32[4,256,8]{1,2,0:T(8,128)S(1)} fusion(s32[8192,4]{0,1:T(4,128)S(1)} %constant_dynamic-slice_fusion.8, f32[1,8192,4,8]{1,0,3,2:T(1,128)S(1)} %constant_dynamic-slice_fusion.7, f32[4,256,8]{1,2,0:T(8,128)S(1)} %get-tuple-element.285, pred[]{:T(512)S(6)} %compare.12), kind=kOutput, calls=%fused_computation.18.clone.1 | convolution fusion | flops 813711360 | bytes 1245185 | tf_op jit(solution)/shard_map/while/body/eval_jaxpr/rsk,rsc->skc/dot_general | solution.py:39
  252.7 10.9 %fusion.22 = f32[4,256,8]{1,2,0:T(8,128)S(1)} fusion(s32[8192,4]{0,1:T(4,128)S(1)} %constant_dynamic-slice_fusion.6, f32[1,8192,4,8]{1,0,3,2:T(1,128)S(1)} %constant_dynamic-slice_fusion.7, f32[4,256,8]{1,2,0:T(8,128)S(1)} %get-tuple-element.283, pred[]{:T(512)S(6)} %compare.12), kind=kOutput, calls=%fused_computation.19.clone.1 | convolution fusion | flops 813711360 | bytes 1245185 | tf_op jit(solution)/shard_map/while/body/eval_jaxpr/rsk,rsc->skc/dot_general | solution.py:39
  263.6 13.5 %fusion.23 = f32[4,256]{1,0:T(4,128)S(1)} fusion(s32[8192,4]{0,1:T(4,128)S(1)} %constant_dynamic-slice_fusion.8), kind=kLoop, calls=%fused_computation.14.clone.1 | loop fusion | flops 25164800 | bytes 135168 | tf_op jit(solution)/shard_map/while/body/eval_jaxpr/reduce_sum | solution.py:46
  277.1 13.6 %fusion.24 = f32[4,256]{1,0:T(4,128)S(1)} fusion(s32[8192,4]{0,1:T(4,128)S(1)} %constant_dynamic-slice_fusion.6), kind=kLoop, calls=%fused_computation.15.clone.1 | loop fusion | flops 25164800 | bytes 135168 | tf_op jit(solution)/shard_map/while/body/eval_jaxpr/reduce_sum | solution.py:46
  291.4 40.0 %all-reduce.3.cloned.1.call-done = (f32[256,32]{0,1:T(8,128)}, f32[256,4]{0,1:T(4,128)}, f32[256,32]{0,1:T(8,128)}, f32[256,4]{0,1:T(4,128)}) async-done(((f32[256,32]{0,1:T(8,128)}, f32[256,4]{0,1:T(4,128)}, f32[256,32]{0,1:T(8,128)}, f32[256,4]{0,1:T(4,128)}), (f32[256,32]{0,1:T(8,128)}, f32[256,4]{0,1:T(4,128)}, f32[256,32]{0,1:T(8,128)}, f32[256,4]{0,1:T(4,128)})) %all-reduce.3.cloned.1.call-update) | async-done | bytes 73744 | tf_op jit(solution)/shard_map/psum | solution.py:60
  332.8 1.4 bitcast_divide_fusion
  (70 shorter events, 17.9 us)
Async XLA Ops:
  7.2 1.2 copy-start
  7.2 4.4 %copy-start.9 = (s32[512]{0:T(512)S(1)}, s32[512]{0:T(512)}, u32[]{:S(2)}) copy-start(s32[512]{0:T(512)} %param.9) | copy-start | bytes 6148
  25.3 2.6 copy-start.7
  25.3 2.6 copy-start.8
  58.7 4.9 %copy-start.1 = (s32[512,128]{1,0:T(8,128)S(1)}, s32[512,128]{1,0:T(8,128)}, u32[]{:S(2)}) copy-start(s32[512,128]{1,0:T(8,128)} %param.12) | copy-start | bytes 786436
  58.7 57.7 %all-to-all-start.2 = ((bf16[128,8,1024]{2,1,0:T(8,128)(2,1)}), bf16[128,8,1024]{2,1,0:T(8,128)(2,1)S(1)}, u32[]{:S(2)}, u32[]{:S(2)}) async-start(bf16[128,8,1024]{2,1,0:T(8,128)(2,1)} %bitcast_select_fusion), calls=%async_computation.2 | async-start | bytes 4194304 | tf_op jit(solution)/shard_map/all_to_all | solution.py:97
  90.7 19.9 %copy-start.2 = (s32[1,512,4]{2,1,0:T(8,128)S(1)}, s32[1,512,4]{2,1,0:T(8,128)}, u32[]{:S(2)}) copy-start(s32[1,512,4]{2,1,0:T(8,128)} %get-tuple-element.194) | copy-start | bytes 24580
  116.3 15.5 %all-to-all-start = ((s32[32,512,4]{1,2,0:T(4,128)}), s32[32,512,4]{1,2,0:T(4,128)S(1)}, u32[]{:S(2)}, u32[]{:S(2)}) async-start(s32[32,512,4]{1,2,0:T(4,128)} %copy.88), calls=%async_computation | async-start | bytes 524288 | tf_op jit(solution)/shard_map/all_to_all | solution.py:14
  131.8 34.0 %all-to-all-start.3 = ((f32[512,32,32]{0,2,1:T(8,128)}), f32[512,32,32]{0,2,1:T(8,128)S(1)}, u32[]{:S(2)}, u32[]{:S(2)}) async-start(f32[512,32,32]{0,2,1:T(8,128)} %bitcast.108), calls=%async_computation.3 | async-start | bytes 4194304 | tf_op jit(solution)/shard_map/all_to_all | solution.py:112
  165.8 13.5 %all-to-all-start.4 = ((s32[512,32,4]{0,2,1:T(4,128)}), s32[512,32,4]{0,2,1:T(4,128)}, u32[]{:S(2)}, u32[]{:S(2)}) async-start(s32[512,32,4]{0,2,1:T(4,128)} %all_to_all.45), calls=%async_computation.4 | async-start | bytes 524288 | tf_op jit(solution)/shard_map/all_to_all | solution.py:114
  170.4 161.0 %all-reduce.3.cloned.1.call-start = ((), (), s32[]{:S(2)}) async-start(), calls=%async_computation.5 | async-start | bytes 147456 | tf_op jit(solution)/shard_map/psum | solution.py:60
  290.7 0.6 copy-start.3
  290.8 0.6 copy-start.4
  290.8 0.6 copy-start.5
  290.8 0.6 copy-start.6
Sparse Core Ops, SparseCore 0:
  291.5 39.8 all-reduce.2
